TPU v7x, 512 devices: a whole 4x8x8 slice. The times are simulated.
512 devices in a mesh: wide: 32 (over y, x_hi, core), blk: 16 (over x_lo, z).
Axes of the slice: x: 4 (x_hi: 2, x_lo: 2; x = x_hi * 2 + x_lo), y: 8, z: 8, core: 2. Of those that a mesh axis runs over, the one named last changes fastest.
Arguments:
- audio: bfloat16 [65536, 1024], P(('wide', 'blk')), may hold values from -1 to 1
- video: bfloat16 [65536, 1024], P(('wide', 'blk')), may hold values from -1 to 1
- owner: int32 [65536, 1], P(('wide', 'blk')), may hold values from 0 to 31; in each aligned block of 128 rows (0 to 127, 128 to 255, ...) at most 8 rows name the same one
- clip_feats: bfloat16 [131072, 1024], P(('wide', 'blk')), may hold values from -48 to 48
- lengths: int32 [131072], P(('wide', 'blk')), may hold values from 1 to 16
- proj_weight: bfloat16 [1024, 1024], replicated, may hold values from -0.1875 to 0.1875
Outputs:
- audio_grad: bfloat16 [65536, 1024], P(('wide', 'blk'))
- feats_grad: bfloat16 [131072, 1024], P(('wide', 'blk'))
- weight_grad: float32 [1024, 1024], P('wide')
Inputs may be any that keep to these rules, and one draw needn't show every extreme that they name: Among the 128 rows of one device, no owner is named more than 8 times, a bound that some block reaches.
All inputs are finite; a program needn't handle non-finite values.
Results may differ from a plain program's by a relative error of at most 0.02.
Values may be sent and summed in bfloat16 or wider, within the bound.
No kernel may reach another device: no remote copies, remote signals or barrier semaphores. Data moves between devices by JAX's collectives and lax.ppermute only.
A program may use at most 64 MiB of HBM per device.

v0:
```python
import jax
import jax.numpy as jnp
from jax import lax
from jax.sharding import Mesh
from jax.sharding import PartitionSpec as P

AXES = ("wide_y", "wide_x", "wide_c", "blk_x", "blk_z")
WIDE = ("wide_y", "wide_x", "wide_c")
BLK = ("blk_x", "blk_z")
BF16 = jnp.bfloat16
F32 = jnp.float32


def swapped(array, axis):
    return lax.ppermute(array, axis, [(0, 1), (1, 0)])


def rows_dot(matrix_a, matrix_b):
    return lax.dot_general(matrix_a, matrix_b, (((1,), (1,)), ((), ())), preferred_element_type=F32)


def cols_dot(matrix_a, matrix_b):
    return lax.dot_general(matrix_a, matrix_b, (((0,), (0,)), ((), ())), preferred_element_type=F32)


def plain_dot(matrix_a, matrix_b):
    return jnp.dot(matrix_a, matrix_b, preferred_element_type=F32)


def gelu_slope(v):
    cdf = 0.5 * (1.0 + lax.erf(v * 0.7071067811865476))
    return cdf + v * (0.3989422804014327 * jnp.exp(-0.5 * v * v))


def pair_coeffs(scores, labels, factor):
    return (factor * (jax.nn.sigmoid(4.0 * scores - 2.0) - labels)).astype(BF16)


def placing_of(owner, slot_count, capacity):
    count = owner.shape[0]
    ids = jnp.arange(count, dtype=jnp.int32)
    peer = owner[:, 0]
    before = (peer[:, None] == peer[None, :]) & (ids[:, None] < ids[None, :])
    target = peer * capacity + jnp.sum(before.astype(jnp.int32), axis=0)
    return (jnp.arange(slot_count, dtype=jnp.int32)[:, None] == target[None, :]).astype(BF16)


def picking_of(core, feature_count):
    half = feature_count // 2
    ny, nx = (lax.axis_size("wide_y"), lax.axis_size("wide_x"))
    bx = lax.axis_size("blk_x")
    share = half // (ny * nx * bx)
    place = jnp.arange(half, dtype=jnp.int32)
    within, rest = (place % share, place // share)
    y, apart = (rest % ny, rest // ny)
    x_wide = apart // bx ^ lax.axis_index("wide_x")
    x_blk = apart % bx ^ lax.axis_index("blk_x")
    feature = (((y * nx + x_wide) * 2 + core) * bx + x_blk) * share + within
    return (jnp.arange(feature_count, dtype=jnp.int32)[:, None] == feature[None, :]).astype(BF16)


def shards(audio, video, owner, clip_feats, lengths, proj_weight):
    clips, features = audio.shape
    blocks = lax.axis_size(BLK)
    factor = 4.0 / blocks
    z, core = (lax.axis_index("blk_z"), lax.axis_index("wide_c"))
    nz = lax.axis_size("blk_z")
    audio_line = lax.all_gather(audio, "blk_z", axis=0, tiled=True)
    video_line = lax.all_gather(video, "blk_z", axis=0, tiled=True)
    peers = lax.axis_size(WIDE)
    slots = clip_feats.shape[0]
    capacity = slots // peers
    length_scale = lax.rsqrt(lengths.astype(F32))[:, None]
    pooled = (clip_feats.astype(F32) * length_scale).astype(BF16)
    pooled_slots = lax.all_to_all(
        pooled.reshape(peers, capacity, features), WIDE, 0, 0, tiled=True
    ).reshape(slots, features)
    both = swapped(jnp.concatenate([video, audio]), "blk_x")
    video_pair = jnp.concatenate([video, both[:clips]])
    audio_pair = jnp.concatenate([audio, both[clips:]])
    slope_own = gelu_slope(plain_dot(pooled, proj_weight))
    placing = placing_of(owner, slots, capacity)
    clip_rows = cols_dot(placing, pooled_slots).astype(BF16)
    row_pair = jnp.concatenate([clip_rows, swapped(clip_rows, "blk_x")])
    slope_pair = gelu_slope(plain_dot(row_pair, proj_weight))
    picked = plain_dot(row_pair, picking_of(core, features)).astype(BF16)
    other = plain_dot(row_pair, picking_of(1 - core, features)).astype(BF16)
    picked = jnp.concatenate([picked, swapped(other, "wide_c")])
    audio_line, slope_pair, picked, slope_own, placing = lax.optimization_barrier(
        (audio_line, slope_pair, picked, slope_own, placing)
    )
    row_ids = jnp.arange(nz * clips, dtype=jnp.int32)[:, None]
    col_ids = jnp.arange(2 * clips, dtype=jnp.int32)[None, :]
    labels = ((row_ids == z * clips + col_ids) & (col_ids < clips)).astype(F32)
    coeffs = pair_coeffs(rows_dot(audio_line, video_pair), labels, factor)
    video_part = cols_dot(coeffs, audio_line)
    pre_part = (video_part * slope_pair).astype(BF16)
    video_part, pre_part = lax.optimization_barrier((video_part, pre_part))
    pre_both = jnp.concatenate([pre_part, swapped(pre_part, "wide_c")])
    ny = lax.axis_size("wide_y")
    share = features // 8
    blocks_of = [cols_dot(picked[:, d * share : (d + 1) * share], pre_both) for d in range(4)]
    summed = blocks_of[0]
    for d in (2, 1, 3):
        pairs = [(place, place ^ d) for place in range(4)]
        summed = summed + lax.ppermute(
            blocks_of[d].astype(BF16), ("wide_x", "blk_x"), pairs
        ).astype(F32)
    summed = summed.astype(BF16)
    arrived = swapped(video_part[clips:].astype(BF16), "blk_x")
    arrived, _ = lax.optimization_barrier((arrived, blocks_of))
    video_grad = (video_part[:clips] + arrived.astype(F32)).astype(BF16)
    packed = plain_dot(placing, video_grad).astype(BF16)
    received = lax.all_to_all(
        packed.reshape(peers, capacity, features), WIDE, 0, 0, tiled=True
    ).reshape(slots, features)
    summed, received = lax.optimization_barrier((summed, received))
    pre_grad = (received.astype(F32) * slope_own).astype(BF16)
    feats_grad = (rows_dot(pre_grad, proj_weight) * length_scale).astype(BF16)
    rows, cols = (summed.shape[0] // ny, features // nz)
    summed = summed.reshape(ny, rows, nz, cols).transpose(0, 2, 1, 3).reshape(ny * nz, rows, cols)
    pieces = lax.all_to_all(summed, ("wide_y", "blk_z"), 0, 0, tiled=True)
    video_line, summed = lax.optimization_barrier((video_line, summed))
    coeffs = pair_coeffs(rows_dot(audio_pair, video_line), labels.T, factor)
    audio_part = plain_dot(coeffs, video_line)
    audio_part, pieces = lax.optimization_barrier((audio_part, pieces))
    arrived = swapped(audio_part[clips:].astype(BF16), "blk_x")
    total = jnp.sum(pieces.astype(F32), axis=0).astype(BF16)
    gathered = lax.all_to_all(
        jnp.broadcast_to(total[None], (blocks, rows, cols)), BLK, 0, 0, tiled=True
    )
    arrived, gathered = lax.optimization_barrier((arrived, gathered))
    audio_grad = (audio_part[:clips] + arrived.astype(F32)).astype(BF16)
    weight_grad = (
        gathered.reshape(-1, nz, rows, cols).transpose(0, 2, 1, 3).reshape(-1, features).astype(F32)
    )
    return (audio_grad, feats_grad, weight_grad)


def solution(mesh):
    finer = Mesh(mesh.devices.reshape(8, 2, 2, 2, 8), AXES)
    rows = P(AXES, None)
    return jax.shard_map(
        shards,
        mesh=finer,
        in_specs=(rows, rows, rows, rows, P(AXES), P()),
        out_specs=(rows, rows, P(WIDE, None)),
        check_vma=False,
    )
```

profile of v0, /device:TPU:2, one launch (start us, length us, event | category | flops | bytes accessed | tf_op | source)
XLA Modules:
  0.0 163.2 jit_solution(10243242646058370700)
XLA Ops:
  7.3 0.7 all-gather.5.cloned.1.call-update
  7.9 0.7 convert_rsqrt_fusion
  8.7 2.0 %fusion.58 = bf16[32,8,1024]{2,1,0:T(8,128)(2,1)} fusion(f32[256]{0:T(256)S(1)} %convert_rsqrt_fusion, bf16[256,1024]{1,0:T(8,128)(2,1)} %param.9), kind=kLoop, calls=%fused_computation.77 | loop fusion | flops 786432 | bytes 1049600 | tf_op jit(solution)/shard_map/reshape | solution.py:76
  10.7 9.1 %all-to-all-start = ((bf16[32,8,1024]{2,1,0:T(8,128)(2,1)}), bf16[32,8,1024]{2,1,0:T(8,128)(2,1)S(1)}, u32[]{:S(2)}, u32[]{:S(2)}) async-start(bf16[32,8,1024]{2,1,0:T(8,128)(2,1)} %fusion.58), calls=%async_computation | async-start | bytes 1048576 | tf_op jit(solution)/shard_map/all_to_all | solution.py:75
  19.8 0.8 pad_maximum_fusion.1
  20.6 3.3 %collective-permute-start = (bf16[256,1024]{1,0:T(8,128)(2,1)}, bf16[256,1024]{1,0:T(8,128)(2,1)S(1)}, u32[]{:S(2)}, u32[]{:S(2)}) collective-permute-start(bf16[256,1024]{1,0:T(8,128)(2,1)} %pad_maximum_fusion.1), channel_id=1, source_target_pairs={{0,8},{8,0},{1,9},{9,1},{2,10},{10,2},{3,11},{11,3},{4,12},{12,4},... | collective-permute-start | bytes 1572872 | tf_op jit(solution)/shard_map/ppermute | solution.py:15
  24.2 3.1 %fusion.29 = f32[256,1024]{1,0:T(8,128)} fusion(bf16[1024,1024]{1,0:T(8,128)(2,1)S(1)} %copy-done, bf16[256,1024]{1,0:T(8,128)(2,1)} %param.9, f32[256]{0:T(256)S(1)} %convert_rsqrt_fusion), kind=kOutput, calls=%fused_computation.38 | convolution fusion | flops 539754496 | bytes 3671040 | tf_op jit(solution)/shard_map/dot_general | solution.py:27
  27.3 10.5 %all-to-all-done = bf16[32,8,1024]{2,1,0:T(8,128)(2,1)S(1)} async-done(((bf16[32,8,1024]{2,1,0:T(8,128)(2,1)}), bf16[32,8,1024]{2,1,0:T(8,128)(2,1)S(1)}, u32[]{:S(2)}, u32[]{:S(2)}) %all-to-all-start) | async-done | bytes 524320 | tf_op jit(solution)/shard_map/all_to_all | solution.py:75
  37.8 0.3 convolution_convert_fusion.1
  38.0 3.3 %collective-permute-start.1 = (bf16[128,1024]{1,0:T(8,128)(2,1)S(1)}, bf16[128,1024]{1,0:T(8,128)(2,1)S(1)}, u32[]{:S(2)}, u32[]{:S(2)}) collective-permute-start(bf16[128,1024]{1,0:T(8,128)(2,1)S(1)} %convolution_convert_fusion.1), channel_id=1, source_target_pairs={{0,8},{8,0},{1,9},{9,1},{2,10},{10,2},{3,11},{11,3},{4,12},{12,4},... | collective-permute-start | bytes 786440 | tf_op jit(solution)/shard_map/ppermute | solution.py:15
  41.4 0.8 fusion.103
  42.2 5.1 %collective-permute-done.1 = bf16[128,1024]{1,0:T(8,128)(2,1)S(1)} collective-permute-done((bf16[128,1024]{1,0:T(8,128)(2,1)S(1)}, bf16[128,1024]{1,0:T(8,128)(2,1)S(1)}, u32[]{:S(2)}, u32[]{:S(2)}) %collective-permute-start.1) | collective-permute-done | bytes 262176 | tf_op jit(solution)/shard_map/ppermute | solution.py:15
  47.4 0.5 fusion.20
  47.9 1.9 %collective-permute-start.2 = (bf16[256,512]{1,0:T(8,128)(2,1)S(1)}, bf16[256,512]{1,0:T(8,128)(2,1)S(1)}, u32[]{:S(2)}, u32[]{:S(2)}) collective-permute-start(bf16[256,512]{1,0:T(8,128)(2,1)S(1)} %fusion.20), channel_id=1, source_target_pairs={{0,16},{16,0},{1,17},{17,1},{2,18},{18,2},{3,19},{19,3},{4,20},{20... | collective-permute-start | bytes 786440 | tf_op jit(solution)/shard_map/ppermute | solution.py:15
  49.9 2.0 %fusion.25 = f32[256,1024]{1,0:T(8,128)} fusion(bf16[1024,1024]{1,0:T(8,128)(2,1)S(1)} %copy-done, bf16[128,1024]{1,0:T(8,128)(2,1)S(1)} %collective-permute-done.1, bf16[128,1024]{1,0:T(8,128)(2,1)S(1)} %convolution_convert_fusion.1), kind=kOutput, calls=%fused_computation.34 | convolution fusion | flops 540016640 | bytes 3670016 | tf_op jit(solution)/shard_map/dot_general | solution.py:27
  51.8 0.5 fusion.21
  52.4 0.8 pad_maximum_fusion.5
  53.2 6.2 %all-gather.5.cloned.1.call-done = bf16[1024,1024]{1,0:T(8,128)(2,1)} async-done(((bf16[128,1024]{1,0:T(8,128)(2,1)}), bf16[1024,1024]{1,0:T(8,128)(2,1)}) %all-gather.5.cloned.1.call-update) | async-done | bytes 2097168 | tf_op jit(solution)/shard_map/all_gather | solution.py:68
  59.5 4.8 %fusion.33 = f32[256,1024]{1,0:T(8,128)S(1)} fusion(bf16[1024,1024]{1,0:T(8,128)(2,1)} %all-gather.5.cloned.1.call-done, bf16[128,1024]{1,0:T(8,128)(2,1)S(1)} %copy-done.3, bf16[128,1024]{1,0:T(8,128)(2,1)} %get-tuple-element.34, s32[256]{0:T(256)S(1)} %iota_add_fusion, pred[256]{0:T(512)(128)(4,1)S(1)} %iota_compare_fusion.13), kind=kOutput, calls=%fused_computation.47 | convolution fusion | flops 1077673984 | bytes 3671296 | tf_op jit(solution)/shard_map/dot_general | solution.py:23
  64.2 1.4 multiply_convert_fusion.1
  65.6 1.9 %collective-permute-start.3 = (bf16[256,1024]{1,0:T(8,128)(2,1)S(1)}, bf16[256,1024]{1,0:T(8,128)(2,1)S(1)}, u32[]{:S(2)}, u32[]{:S(2)}) collective-permute-start(bf16[256,1024]{1,0:T(8,128)(2,1)S(1)} %multiply_convert_fusion.1), channel_id=1, source_target_pairs={{0,16},{16,0},{1,17},{17,1},{2,18},{18,2},{3,19},{19,3},{4,20},{20... | collective-permute-start | bytes 1572872 | tf_op jit(solution)/shard_map/ppermute | solution.py:15
  67.6 2.4 %collective-permute-start.7 = (bf16[128,1024]{1,0:T(8,128)(2,1)S(1)}, bf16[128,1024]{1,0:T(8,128)(2,1)S(1)}, u32[]{:S(2)}, u32[]{:S(2)}) collective-permute-start(bf16[128,1024]{1,0:T(8,128)(2,1)S(1)} %slice.60), channel_id=1, source_target_pairs={{0,8},{8,0},{1,9},{9,1},{2,10},{10,2},{3,11},{11,3},{4,12},{12,4},... | collective-permute-start | bytes 786440 | tf_op jit(solution)/shard_map/ppermute | solution.py:15
  70.2 1.0 fusion.64
  71.2 1.1 fusion.66
  72.3 1.0 fusion.62
  73.4 1.0 fusion.60
  74.4 3.8 %collective-permute-done.7 = bf16[128,1024]{1,0:T(8,128)(2,1)S(1)} collective-permute-done((bf16[128,1024]{1,0:T(8,128)(2,1)S(1)}, bf16[128,1024]{1,0:T(8,128)(2,1)S(1)}, u32[]{:S(2)}, u32[]{:S(2)}) %collective-permute-start.7) | collective-permute-done | bytes 262176 | tf_op jit(solution)/shard_map/ppermute | solution.py:15
  78.2 1.1 fusion.19
  79.3 8.8 %all-to-all-start.1 = ((bf16[32,8,1024]{2,1,0:T(8,128)(2,1)}), bf16[32,8,1024]{2,1,0:T(8,128)(2,1)S(1)}, u32[]{:S(2)}, u32[]{:S(2)}) async-start(bf16[32,8,1024]{2,1,0:T(8,128)(2,1)} %fusion.19), calls=%async_computation.1 | async-start | bytes 1048576 | tf_op jit(solution)/shard_map/all_to_all | solution.py:114
  88.1 5.2 %collective-permute-start.4 = (bf16[128,1024]{1,0:T(8,128)(2,1)}, bf16[128,1024]{1,0:T(8,128)(2,1)S(1)}, u32[]{:S(2)}, u32[]{:S(2)}) collective-permute-start(bf16[128,1024]{1,0:T(8,128)(2,1)} %fusion.64), channel_id=1, source_target_pairs={{0,32},{8,40},{32,0},{40,8},{1,33},{9,41},{33,1},{41,9},{2,34},{10... | collective-permute-start | bytes 786440 | tf_op jit(solution)/shard_map/ppermute | solution.py:106
  93.3 3.4 %collective-permute-start.5 = (bf16[128,1024]{1,0:T(8,128)(2,1)}, bf16[128,1024]{1,0:T(8,128)(2,1)S(1)}, u32[]{:S(2)}, u32[]{:S(2)}) collective-permute-start(bf16[128,1024]{1,0:T(8,128)(2,1)} %fusion.62), channel_id=1, source_target_pairs={{0,8},{8,0},{32,40},{40,32},{1,9},{9,1},{33,41},{41,33},{2,10},{10... | collective-permute-start | bytes 786440 | tf_op jit(solution)/shard_map/ppermute | solution.py:106
  96.7 1.9 %collective-permute-start.6 = (bf16[128,1024]{1,0:T(8,128)(2,1)}, bf16[128,1024]{1,0:T(8,128)(2,1)S(1)}, u32[]{:S(2)}, u32[]{:S(2)}) collective-permute-start(bf16[128,1024]{1,0:T(8,128)(2,1)} %fusion.60), channel_id=1, source_target_pairs={{0,40},{8,32},{32,8},{40,0},{1,41},{9,33},{33,9},{41,1},{2,42},{10... | collective-permute-start | bytes 786440 | tf_op jit(solution)/shard_map/ppermute | solution.py:106
  98.6 6.7 %collective-permute-done.4 = bf16[128,1024]{1,0:T(8,128)(2,1)S(1)} collective-permute-done((bf16[128,1024]{1,0:T(8,128)(2,1)}, bf16[128,1024]{1,0:T(8,128)(2,1)S(1)}, u32[]{:S(2)}, u32[]{:S(2)}) %collective-permute-start.4) | collective-permute-done | bytes 262176 | tf_op jit(solution)/shard_map/ppermute | solution.py:106
  105.3 4.9 %collective-permute-done.5 = bf16[128,1024]{1,0:T(8,128)(2,1)S(1)} collective-permute-done((bf16[128,1024]{1,0:T(8,128)(2,1)}, bf16[128,1024]{1,0:T(8,128)(2,1)S(1)}, u32[]{:S(2)}, u32[]{:S(2)}) %collective-permute-start.5) | collective-permute-done | bytes 262176 | tf_op jit(solution)/shard_map/ppermute | solution.py:106
  110.2 0.5 collective-permute-done.6
  110.7 1.2 add_convert_fusion.2
  112.0 0.8 copy.12
  112.7 9.2 %all-to-all-start.2 = ((bf16[64,16,128]{2,1,0:T(8,128)(2,1)}), bf16[64,16,128]{2,1,0:T(8,128)(2,1)S(1)}, u32[]{:S(2)}, u32[]{:S(2)}) async-start(bf16[64,16,128]{2,1,0:T(8,128)(2,1)} %bitcast.6), calls=%async_computation.2 | async-start | bytes 524288 | tf_op jit(solution)/shard_map/all_to_all | solution.py:122
  121.9 4.7 %fusion.35 = f32[256,1024]{1,0:T(8,128)} fusion(bf16[1024,1024]{1,0:T(8,128)(2,1)} %all-gather.3.cloned.1.call-done, bf16[128,1024]{1,0:T(8,128)(2,1)S(1)} %copy-done.6, bf16[128,1024]{1,0:T(8,128)(2,1)S(1)} %copy-done.5, s32[256]{0:T(256)S(1)} %iota_add_fusion, pred[256]{0:T(512)(128)(4,1)S(1)} %iota_compare_fusion.13), kind=kOutput, calls=%fused_computation.49 | convolution fusion | flops 1077673984 | bytes 3671296 | tf_op jit(solution)/shard_map/dot_general | solution.py:27
  126.6 10.4 %all-to-all-done.2 = bf16[64,16,128]{2,1,0:T(8,128)(2,1)S(1)} async-done(((bf16[64,16,128]{2,1,0:T(8,128)(2,1)}), bf16[64,16,128]{2,1,0:T(8,128)(2,1)S(1)}, u32[]{:S(2)}, u32[]{:S(2)}) %all-to-all-start.2) | async-done | bytes 262176 | tf_op jit(solution)/shard_map/all_to_all | solution.py:122
  137.0 1.1 slice.59
  138.1 3.4 %collective-permute-start.8 = (bf16[128,1024]{1,0:T(8,128)(2,1)S(1)}, bf16[128,1024]{1,0:T(8,128)(2,1)S(1)}, u32[]{:S(2)}, u32[]{:S(2)}) collective-permute-start(bf16[128,1024]{1,0:T(8,128)(2,1)S(1)} %slice.59), channel_id=1, source_target_pairs={{0,8},{8,0},{1,9},{9,1},{2,10},{10,2},{3,11},{11,3},{4,12},{12,4},... | collective-permute-start | bytes 786440 | tf_op jit(solution)/shard_map/ppermute | solution.py:15
  141.6 0.6 broadcast_in_dim.2
  142.2 4.4 %all-to-all-start.3 = ((bf16[16,16,128]{2,1,0:T(8,128)(2,1)}), bf16[16,16,128]{2,1,0:T(8,128)(2,1)S(1)}, u32[]{:S(2)}, u32[]{:S(2)}) async-start(bf16[16,16,128]{2,1,0:T(8,128)(2,1)} %broadcast_in_dim.2), calls=%async_computation.3 | async-start | bytes 131072 | tf_op jit(solution)/shard_map/all_to_all | solution.py:129
  146.6 2.8 %fusion.18 = bf16[256,1024]{1,0:T(8,128)(2,1)} fusion(bf16[1024,1024]{1,0:T(8,128)(2,1)S(1)} %copy-done, f32[256,1024]{1,0:T(8,128)} %fusion.29, bf16[256,1024]{1,0:T(8,128)(2,1)S(1)} %bitcast.37, f32[256]{0:T(256)S(1)} %convert_rsqrt_fusion), kind=kOutput, calls=%fused_computation.25 | convolution fusion | flops 538181632 | bytes 4195328 | tf_op jit(solution)/shard_map/dot_general | solution.py:19
  149.3 4.5 %all-to-all-done.3 = bf16[16,16,128]{2,1,0:T(8,128)(2,1)S(1)} async-done(((bf16[16,16,128]{2,1,0:T(8,128)(2,1)}), bf16[16,16,128]{2,1,0:T(8,128)(2,1)S(1)}, u32[]{:S(2)}, u32[]{:S(2)}) %all-to-all-start.3) | async-done | bytes 65568 | tf_op jit(solution)/shard_map/all_to_all | solution.py:129
  153.9 0.7 copy.17
  154.6 1.8 %add_convert_fusion = bf16[128,1024]{1,0:T(8,128)(2,1)} fusion(bf16[128,1024]{1,0:T(8,128)(2,1)S(1)} %collective-permute-done.8, f32[256,1024]{1,0:T(8,128)} %fusion.35), kind=kLoop, calls=%fused_computation.61 | loop fusion | flops 393216 | bytes 1048576 | tf_op jit(solution)/shard_map/convert_element_type | solution.py:133
  (39 shorter events, 0.6 us)
Async XLA Ops:
  7.2 17.0 %copy-start = (bf16[1024,1024]{1,0:T(8,128)(2,1)S(1)}, bf16[1024,1024]{1,0:T(8,128)(2,1)}, u32[]{:S(2)}) copy-start(bf16[1024,1024]{1,0:T(8,128)(2,1)} %param.11) | copy-start | bytes 6291460
  7.2 12.6 %copy-start.4 = (bf16[128,1024]{1,0:T(8,128)(2,1)S(1)}, bf16[128,1024]{1,0:T(8,128)(2,1)}, u32[]{:S(2)}) copy-start(bf16[128,1024]{1,0:T(8,128)(2,1)} %param.6) | copy-start | bytes 786436
  7.2 12.6 %copy-start.2 = (bf16[128,1024]{1,0:T(8,128)(2,1)S(1)}, bf16[128,1024]{1,0:T(8,128)(2,1)}, u32[]{:S(2)}) copy-start(bf16[128,1024]{1,0:T(8,128)(2,1)} %param.7) | copy-start | bytes 786436
  7.2 16.8 %copy-start.7 = (s32[128,1]{0,1:T(1,128)S(1)}, s32[128,1]{0,1:T(1,128)}, u32[]{:S(2)}) copy-start(s32[128,1]{0,1:T(1,128)} %param.8) | copy-start | bytes 1540
  7.2 52.2 %all-gather.5.cloned.1.call-start = ((), (), s32[]{:S(2)}) async-start(), calls=%async_computation.5 | async-start | bytes 2359296 | tf_op jit(solution)/shard_map/all_gather | solution.py:68
  10.7 27.1 %all-to-all-start = ((bf16[32,8,1024]{2,1,0:T(8,128)(2,1)}), bf16[32,8,1024]{2,1,0:T(8,128)(2,1)S(1)}, u32[]{:S(2)}, u32[]{:S(2)}) async-start(bf16[32,8,1024]{2,1,0:T(8,128)(2,1)} %fusion.58), calls=%async_computation | async-start | bytes 1048576 | tf_op jit(solution)/shard_map/all_to_all | solution.py:75
  19.7 102.2 %all-gather.3.cloned.1.call-start = ((), (), s32[]{:S(2)}) async-start(), calls=%async_computation.4 | async-start | bytes 2359296 | tf_op jit(solution)/shard_map/all_gather | solution.py:69
  20.6 20.8 %collective-permute-start = (bf16[256,1024]{1,0:T(8,128)(2,1)}, bf16[256,1024]{1,0:T(8,128)(2,1)S(1)}, u32[]{:S(2)}, u32[]{:S(2)}) collective-permute-start(bf16[256,1024]{1,0:T(8,128)(2,1)} %pad_maximum_fusion.1), channel_id=1, source_target_pairs={{0,8},{8,0},{1,9},{9,1},{2,10},{10,2},{3,11},{11,3},{4,12},{12,4},... | collective-permute-start | bytes 1572872 | tf_op jit(solution)/shard_map/ppermute | solution.py:15
  38.0 9.4 %collective-permute-start.1 = (bf16[128,1024]{1,0:T(8,128)(2,1)S(1)}, bf16[128,1024]{1,0:T(8,128)(2,1)S(1)}, u32[]{:S(2)}, u32[]{:S(2)}) collective-permute-start(bf16[128,1024]{1,0:T(8,128)(2,1)S(1)} %convolution_convert_fusion.1), channel_id=1, source_target_pairs={{0,8},{8,0},{1,9},{9,1},{2,10},{10,2},{3,11},{11,3},{4,12},{12,4},... | collective-permute-start | bytes 786440 | tf_op jit(solution)/shard_map/ppermute | solution.py:15
  47.9 4.4 %collective-permute-start.2 = (bf16[256,512]{1,0:T(8,128)(2,1)S(1)}, bf16[256,512]{1,0:T(8,128)(2,1)S(1)}, u32[]{:S(2)}, u32[]{:S(2)}) collective-permute-start(bf16[256,512]{1,0:T(8,128)(2,1)S(1)} %fusion.20), channel_id=1, source_target_pairs={{0,16},{16,0},{1,17},{17,1},{2,18},{18,2},{3,19},{19,3},{4,20},{20... | collective-permute-start | bytes 786440 | tf_op jit(solution)/shard_map/ppermute | solution.py:15
  51.8 7.6 %copy-start.3 = (bf16[128,1024]{1,0:T(8,128)(2,1)S(1)}, bf16[128,1024]{1,0:T(8,128)(2,1)}, u32[]{:S(2)}) copy-start(bf16[128,1024]{1,0:T(8,128)(2,1)} %param.7) | copy-start | bytes 786436
  64.2 5.9 %copy-start.1 = (bf16[512,512]{1,0:T(8,128)(2,1)S(1)}, bf16[512,512]{1,0:T(8,128)(2,1)}, u32[]{:S(2)}) copy-start(bf16[512,512]{1,0:T(8,128)(2,1)} %pad_maximum_fusion.5) | copy-start | bytes 1572868
  65.6 4.5 %collective-permute-start.3 = (bf16[256,1024]{1,0:T(8,128)(2,1)S(1)}, bf16[256,1024]{1,0:T(8,128)(2,1)S(1)}, u32[]{:S(2)}, u32[]{:S(2)}) collective-permute-start(bf16[256,1024]{1,0:T(8,128)(2,1)S(1)} %multiply_convert_fusion.1), channel_id=1, source_target_pairs={{0,16},{16,0},{1,17},{17,1},{2,18},{18,2},{3,19},{19,3},{4,20},{20... | collective-permute-start | bytes 1572872 | tf_op jit(solution)/shard_map/ppermute | solution.py:15
  67.6 10.6 %collective-permute-start.7 = (bf16[128,1024]{1,0:T(8,128)(2,1)S(1)}, bf16[128,1024]{1,0:T(8,128)(2,1)S(1)}, u32[]{:S(2)}, u32[]{:S(2)}) collective-permute-start(bf16[128,1024]{1,0:T(8,128)(2,1)S(1)} %slice.60), channel_id=1, source_target_pairs={{0,8},{8,0},{1,9},{9,1},{2,10},{10,2},{3,11},{11,3},{4,12},{12,4},... | collective-permute-start | bytes 786440 | tf_op jit(solution)/shard_map/ppermute | solution.py:15
  79.3 42.6 %copy-start.5 = (bf16[128,1024]{1,0:T(8,128)(2,1)S(1)}, bf16[128,1024]{1,0:T(8,128)(2,1)}, u32[]{:S(2)}) copy-start(bf16[128,1024]{1,0:T(8,128)(2,1)} %param.6) | copy-start | bytes 786436
  79.3 42.6 %copy-start.6 = (bf16[128,1024]{1,0:T(8,128)(2,1)S(1)}, bf16[128,1024]{1,0:T(8,128)(2,1)}, u32[]{:S(2)}) copy-start(bf16[128,1024]{1,0:T(8,128)(2,1)} %get-tuple-element.33) | copy-start | bytes 786436
  79.3 32.6 %all-to-all-start.1 = ((bf16[32,8,1024]{2,1,0:T(8,128)(2,1)}), bf16[32,8,1024]{2,1,0:T(8,128)(2,1)S(1)}, u32[]{:S(2)}, u32[]{:S(2)}) async-start(bf16[32,8,1024]{2,1,0:T(8,128)(2,1)} %fusion.19), calls=%async_computation.1 | async-start | bytes 1048576 | tf_op jit(solution)/shard_map/all_to_all | solution.py:114
  88.1 17.2 %collective-permute-start.4 = (bf16[128,1024]{1,0:T(8,128)(2,1)}, bf16[128,1024]{1,0:T(8,128)(2,1)S(1)}, u32[]{:S(2)}, u32[]{:S(2)}) collective-permute-start(bf16[128,1024]{1,0:T(8,128)(2,1)} %fusion.64), channel_id=1, source_target_pairs={{0,32},{8,40},{32,0},{40,8},{1,33},{9,41},{33,1},{41,9},{2,34},{10... | collective-permute-start | bytes 786440 | tf_op jit(solution)/shard_map/ppermute | solution.py:106
  93.3 16.9 %collective-permute-start.5 = (bf16[128,1024]{1,0:T(8,128)(2,1)}, bf16[128,1024]{1,0:T(8,128)(2,1)S(1)}, u32[]{:S(2)}, u32[]{:S(2)}) collective-permute-start(bf16[128,1024]{1,0:T(8,128)(2,1)} %fusion.62), channel_id=1, source_target_pairs={{0,8},{8,0},{32,40},{40,32},{1,9},{9,1},{33,41},{41,33},{2,10},{10... | collective-permute-start | bytes 786440 | tf_op jit(solution)/shard_map/ppermute | solution.py:106
  96.7 14.0 %collective-permute-start.6 = (bf16[128,1024]{1,0:T(8,128)(2,1)}, bf16[128,1024]{1,0:T(8,128)(2,1)S(1)}, u32[]{:S(2)}, u32[]{:S(2)}) collective-permute-start(bf16[128,1024]{1,0:T(8,128)(2,1)} %fusion.60), channel_id=1, source_target_pairs={{0,40},{8,32},{32,8},{40,0},{1,41},{9,33},{33,9},{41,1},{2,42},{10... | collective-permute-start | bytes 786440 | tf_op jit(solution)/shard_map/ppermute | solution.py:106
  112.7 24.3 %all-to-all-start.2 = ((bf16[64,16,128]{2,1,0:T(8,128)(2,1)}), bf16[64,16,128]{2,1,0:T(8,128)(2,1)S(1)}, u32[]{:S(2)}, u32[]{:S(2)}) async-start(bf16[64,16,128]{2,1,0:T(8,128)(2,1)} %bitcast.6), calls=%async_computation.2 | async-start | bytes 524288 | tf_op jit(solution)/shard_map/all_to_all | solution.py:122
  138.1 15.7 %collective-permute-start.8 = (bf16[128,1024]{1,0:T(8,128)(2,1)S(1)}, bf16[128,1024]{1,0:T(8,128)(2,1)S(1)}, u32[]{:S(2)}, u32[]{:S(2)}) collective-permute-start(bf16[128,1024]{1,0:T(8,128)(2,1)S(1)} %slice.59), channel_id=1, source_target_pairs={{0,8},{8,0},{1,9},{9,1},{2,10},{10,2},{3,11},{11,3},{4,12},{12,4},... | collective-permute-start | bytes 786440 | tf_op jit(solution)/shard_map/ppermute | solution.py:15
  142.2 11.6 %all-to-all-start.3 = ((bf16[16,16,128]{2,1,0:T(8,128)(2,1)}), bf16[16,16,128]{2,1,0:T(8,128)(2,1)S(1)}, u32[]{:S(2)}, u32[]{:S(2)}) async-start(bf16[16,16,128]{2,1,0:T(8,128)(2,1)} %broadcast_in_dim.2), calls=%async_computation.3 | async-start | bytes 131072 | tf_op jit(solution)/shard_map/all_to_all | solution.py:129
Sparse Core Ops, SparseCore 0:
  10.1 49.2 all-gather.4
  61.5 42.7 all-gather.2
where the time goes:
time: 164 us; the launch traced here: 163 us
  starting transfers between devices  58.2 us (35%)
  waiting for transfers between devices  53.4 us (33%)
  matrix products  23.9 us (15%)
  between operations  14.4 us (9%)
  other arithmetic  9.03 us (6%)
  local copies, waits for them, and re-layouts  4.21 us (3%)
    ppermute x6, starting transfers between devices, swapped(): return lax.ppermute(array, axis, [(0, 1), (1, 0)])  16.3 us
    ppermute x3, waiting for transfers between devices, shards(): lax.ppermute(blocks_of[d].astype(BF16), ('wide_x', 'blk_x'), pairs)  12.1 us
    dot_general x6, matrix products, plain_dot(): return jnp.dot(matrix_a, matrix_b, preferred_element_type=F32)  11.9 us
    ppermute x3, starting transfers between devices, shards(): lax.ppermute(blocks_of[d].astype(BF16), ('wide_x', 'blk_x'), pairs)  10.5 us
    all_to_all x1, waiting for transfers between devices, shards(): lax.all_to_all(pooled.reshape(peers, capacity, features), WIDE, 0, 0, til...  10.5 us
    all_to_all x1, waiting for transfers between devices, shards(): pieces = lax.all_to_all(summed, ('wide_y', 'blk_z'), 0, 0, tiled=True)  10.4 us
    dot_general x6, matrix products, cols_dot(): lax.dot_general(matrix_a, matrix_b, (((0,), (0,)), ((), ())), preferred_e...  9.3 us
    all_to_all x1, starting transfers between devices, shards(): pieces = lax.all_to_all(summed, ('wide_y', 'blk_z'), 0, 0, tiled=True)  9.17 us
  transfers between devices with their start and end apart: 15, of which 9 were waited for; matrix products, arithmetic and copies ran while one was open for 21% of the time, Pallas kernels for 0%

commit v1 on v0

--- a/solution.py
+++ b/solution.py
@@ -65,8 +65,11 @@
     factor = 4.0 / blocks
     z, core = (lax.axis_index("blk_z"), lax.axis_index("wide_c"))
     nz = lax.axis_size("blk_z")
-    audio_line = lax.all_gather(audio, "blk_z", axis=0, tiled=True)
-    video_line = lax.all_gather(video, "blk_z", axis=0, tiled=True)
+    audio_line, video_line = jnp.split(
+        lax.all_gather(jnp.concatenate([audio, video], axis=1), "blk_z", axis=0, tiled=True),
+        [audio.shape[1]],
+        axis=1,
+    )
     peers = lax.axis_size(WIDE)
     slots = clip_feats.shape[0]
     capacity = slots // peers

time: 164 us -> 184 us (1.12)
  the two profiles are of different devices: /device:TPU:2 before, /device:TPU:4 now
where the time goes in v1:
time: 184 us; the launch traced here: 183 us
  waiting for transfers between devices  65.9 us (36%)
  starting transfers between devices  58.7 us (32%)
  matrix products  24 us (13%)
  between operations  14.4 us (8%)
  other arithmetic  11 us (6%)
  local copies, waits for them, and re-layouts  8.87 us (5%)
    all_gather x1, waiting for transfers between devices, shards(): lax.all_gather(jnp.concatenate([audio, video], axis=1), 'blk_z', axis=0,...  18.2 us
    ppermute x6, starting transfers between devices, swapped(): return lax.ppermute(array, axis, [(0, 1), (1, 0)])  16.5 us
    ppermute x3, waiting for transfers between devices, shards(): lax.ppermute(blocks_of[d].astype(BF16), ('wide_x', 'blk_x'), pairs)  12.7 us
    dot_general x6, matrix products, plain_dot(): return jnp.dot(matrix_a, matrix_b, preferred_element_type=F32)  11.9 us
    all_to_all x1, waiting for transfers between devices, shards(): lax.all_to_all(pooled.reshape(peers, capacity, features), WIDE, 0, 0, til...  10.4 us
    all_to_all x1, starting transfers between devices, shards(): lax.all_to_all(pooled.reshape(peers, capacity, features), WIDE, 0, 0, til...  10.2 us
    all_to_all x1, waiting for transfers between devices, shards(): pieces = lax.all_to_all(summed, ('wide_y', 'blk_z'), 0, 0, tiled=True)  10.2 us
    all_to_all x1, starting transfers between devices, shards(): lax.all_to_all(packed.reshape(peers, capacity, features), WIDE, 0, 0, til...  9.99 us
  transfers between devices with their start and end apart: 14, of which 10 were waited for; matrix products, arithmetic and copies ran while one was open for 14% of the time, Pallas kernels for 0%

profile of v1, /device:TPU:4, one launch (start us, length us, event | category | flops | bytes accessed | tf_op | source)
XLA Modules:
  0.0 182.8 jit_solution(4861258021265070967)
XLA Ops:
  7.2 2.0 %pad_maximum_fusion.4 = bf16[128,2048]{1,0:T(8,128)(2,1)} fusion(bf16[128,1024]{1,0:T(8,128)(2,1)} %param.7, bf16[128,1024]{1,0:T(8,128)(2,1)} %param.6), kind=kLoop, calls=%fused_computation.57 | loop fusion | flops 1048576 | bytes 1048576 | tf_op jit(solution)/shard_map/concatenate | solution.py:69
  9.3 0.7 convert_rsqrt_fusion
  10.0 2.0 %fusion.58 = bf16[32,8,1024]{2,1,0:T(8,128)(2,1)} fusion(f32[256]{0:T(256)S(1)} %convert_rsqrt_fusion, bf16[256,1024]{1,0:T(8,128)(2,1)} %param.9), kind=kLoop, calls=%fused_computation.78 | loop fusion | flops 786432 | bytes 1049600 | tf_op jit(solution)/shard_map/reshape | solution.py:79
  12.0 10.2 %all-to-all-start = ((bf16[32,8,1024]{2,1,0:T(8,128)(2,1)}), bf16[32,8,1024]{2,1,0:T(8,128)(2,1)S(1)}, u32[]{:S(2)}, u32[]{:S(2)}) async-start(bf16[32,8,1024]{2,1,0:T(8,128)(2,1)} %fusion.58), calls=%async_computation | async-start | bytes 1048576 | tf_op jit(solution)/shard_map/all_to_all | solution.py:78
  22.2 0.8 pad_maximum_fusion.1
  23.0 3.1 %collective-permute-start = (bf16[256,1024]{1,0:T(8,128)(2,1)}, bf16[256,1024]{1,0:T(8,128)(2,1)S(1)}, u32[]{:S(2)}, u32[]{:S(2)}) collective-permute-start(bf16[256,1024]{1,0:T(8,128)(2,1)} %pad_maximum_fusion.1), channel_id=1, source_target_pairs={{0,8},{8,0},{1,9},{9,1},{2,10},{10,2},{3,11},{11,3},{4,12},{12,4},... | collective-permute-start | bytes 1572872 | tf_op jit(solution)/shard_map/ppermute | solution.py:15
  26.3 3.1 %fusion.29 = f32[256,1024]{1,0:T(8,128)} fusion(bf16[1024,1024]{1,0:T(8,128)(2,1)S(1)} %copy-done, bf16[256,1024]{1,0:T(8,128)(2,1)} %param.9, f32[256]{0:T(256)S(1)} %convert_rsqrt_fusion), kind=kOutput, calls=%fused_computation.38 | convolution fusion | flops 539754496 | bytes 3671040 | tf_op jit(solution)/shard_map/dot_general | solution.py:27
  29.5 10.4 %all-to-all-done = bf16[32,8,1024]{2,1,0:T(8,128)(2,1)S(1)} async-done(((bf16[32,8,1024]{2,1,0:T(8,128)(2,1)}), bf16[32,8,1024]{2,1,0:T(8,128)(2,1)S(1)}, u32[]{:S(2)}, u32[]{:S(2)}) %all-to-all-start) | async-done | bytes 524320 | tf_op jit(solution)/shard_map/all_to_all | solution.py:78
  40.2 3.1 %collective-permute-start.1 = (bf16[128,1024]{1,0:T(8,128)(2,1)S(1)}, bf16[128,1024]{1,0:T(8,128)(2,1)S(1)}, u32[]{:S(2)}, u32[]{:S(2)}) collective-permute-start(bf16[128,1024]{1,0:T(8,128)(2,1)S(1)} %convolution_convert_fusion.1), channel_id=1, source_target_pairs={{0,8},{8,0},{1,9},{9,1},{2,10},{10,2},{3,11},{11,3},{4,12},{12,4},... | collective-permute-start | bytes 786440 | tf_op jit(solution)/shard_map/ppermute | solution.py:15
  43.6 0.8 fusion.104
  44.4 5.1 %collective-permute-done.1 = bf16[128,1024]{1,0:T(8,128)(2,1)S(1)} collective-permute-done((bf16[128,1024]{1,0:T(8,128)(2,1)S(1)}, bf16[128,1024]{1,0:T(8,128)(2,1)S(1)}, u32[]{:S(2)}, u32[]{:S(2)}) %collective-permute-start.1) | collective-permute-done | bytes 262176 | tf_op jit(solution)/shard_map/ppermute | solution.py:15
  49.5 0.5 fusion.20
  50.1 1.9 %collective-permute-start.2 = (bf16[256,512]{1,0:T(8,128)(2,1)S(1)}, bf16[256,512]{1,0:T(8,128)(2,1)S(1)}, u32[]{:S(2)}, u32[]{:S(2)}) collective-permute-start(bf16[256,512]{1,0:T(8,128)(2,1)S(1)} %fusion.20), channel_id=1, source_target_pairs={{0,16},{16,0},{1,17},{17,1},{2,18},{18,2},{3,19},{19,3},{4,20},{20... | collective-permute-start | bytes 786440 | tf_op jit(solution)/shard_map/ppermute | solution.py:15
  52.0 2.0 %fusion.25 = f32[256,1024]{1,0:T(8,128)} fusion(bf16[1024,1024]{1,0:T(8,128)(2,1)S(1)} %copy-done, bf16[128,1024]{1,0:T(8,128)(2,1)S(1)} %collective-permute-done.1, bf16[128,1024]{1,0:T(8,128)(2,1)S(1)} %convolution_convert_fusion.1), kind=kOutput, calls=%fused_computation.34 | convolution fusion | flops 540016640 | bytes 3670016 | tf_op jit(solution)/shard_map/dot_general | solution.py:27
  54.0 0.5 fusion.21
  54.6 0.8 pad_maximum_fusion.6
  55.4 18.2 %all-gather.2.cloned.1.call-done = bf16[1024,2048]{1,0:T(8,128)(2,1)} async-done(((bf16[128,2048]{1,0:T(8,128)(2,1)}), bf16[1024,2048]{1,0:T(8,128)(2,1)}) %all-gather.2.cloned.1.call-update) | async-done | bytes 4194320 | tf_op jit(solution)/shard_map/all_gather | solution.py:69
  73.6 4.7 %fusion.103 = (bf16[1024,1024]{1,0:T(8,128)(2,1)}, bf16[1024,1024]{1,0:T(8,128)(2,1)}) fusion(bf16[1024,2048]{1,0:T(8,128)(2,1)} %all-gather.2.cloned.1.call-done), kind=kLoop, calls=%fused_computation.151 | loop fusion | bytes 8388608 | tf_op jit(solution)/shard_map/split | solution.py:68
  78.3 4.8 %fusion.33 = f32[256,1024]{1,0:T(8,128)S(1)} fusion(bf16[1024,1024]{1,0:T(8,128)(2,1)} %get-tuple-element.19, bf16[128,1024]{1,0:T(8,128)(2,1)S(1)} %copy-done.2, bf16[128,1024]{1,0:T(8,128)(2,1)} %get-tuple-element.36, s32[256]{0:T(256)S(1)} %iota_add_fusion, pred[256]{0:T(512)(128)(4,1)S(1)} %iota_compare_fusion.13), kind=kOutput, calls=%fused_computation.47 | convolution fusion | flops 1077673984 | bytes 3671296 | tf_op jit(solution)/shard_map/dot_general | solution.py:23
  83.0 1.4 multiply_convert_fusion.1
  84.5 1.9 %collective-permute-start.3 = (bf16[256,1024]{1,0:T(8,128)(2,1)S(1)}, bf16[256,1024]{1,0:T(8,128)(2,1)S(1)}, u32[]{:S(2)}, u32[]{:S(2)}) collective-permute-start(bf16[256,1024]{1,0:T(8,128)(2,1)S(1)} %multiply_convert_fusion.1), channel_id=1, source_target_pairs={{0,16},{16,0},{1,17},{17,1},{2,18},{18,2},{3,19},{19,3},{4,20},{20... | collective-permute-start | bytes 1572872 | tf_op jit(solution)/shard_map/ppermute | solution.py:15
  86.4 3.1 %collective-permute-start.7 = (bf16[128,1024]{1,0:T(8,128)(2,1)S(1)}, bf16[128,1024]{1,0:T(8,128)(2,1)S(1)}, u32[]{:S(2)}, u32[]{:S(2)}) collective-permute-start(bf16[128,1024]{1,0:T(8,128)(2,1)S(1)} %slice.60), channel_id=1, source_target_pairs={{0,8},{8,0},{1,9},{9,1},{2,10},{10,2},{3,11},{11,3},{4,12},{12,4},... | collective-permute-start | bytes 786440 | tf_op jit(solution)/shard_map/ppermute | solution.py:15
  89.6 1.1 fusion.60
  90.7 1.1 fusion.66
  91.8 1.0 fusion.62
  92.8 1.0 fusion.64
  93.9 3.2 %collective-permute-done.7 = bf16[128,1024]{1,0:T(8,128)(2,1)S(1)} collective-permute-done((bf16[128,1024]{1,0:T(8,128)(2,1)S(1)}, bf16[128,1024]{1,0:T(8,128)(2,1)S(1)}, u32[]{:S(2)}, u32[]{:S(2)}) %collective-permute-start.7) | collective-permute-done | bytes 262176 | tf_op jit(solution)/shard_map/ppermute | solution.py:15
  97.0 1.1 fusion.19
  98.1 10.0 %all-to-all-start.1 = ((bf16[32,8,1024]{2,1,0:T(8,128)(2,1)}), bf16[32,8,1024]{2,1,0:T(8,128)(2,1)S(1)}, u32[]{:S(2)}, u32[]{:S(2)}) async-start(bf16[32,8,1024]{2,1,0:T(8,128)(2,1)} %fusion.19), calls=%async_computation.1 | async-start | bytes 1048576 | tf_op jit(solution)/shard_map/all_to_all | solution.py:117
  108.1 1.9 %collective-permute-start.6 = (bf16[128,1024]{1,0:T(8,128)(2,1)}, bf16[128,1024]{1,0:T(8,128)(2,1)S(1)}, u32[]{:S(2)}, u32[]{:S(2)}) collective-permute-start(bf16[128,1024]{1,0:T(8,128)(2,1)} %fusion.60), channel_id=1, source_target_pairs={{0,40},{8,32},{32,8},{40,0},{1,41},{9,33},{33,9},{41,1},{2,42},{10... | collective-permute-start | bytes 786440 | tf_op jit(solution)/shard_map/ppermute | solution.py:109
  110.1 3.3 %collective-permute-start.5 = (bf16[128,1024]{1,0:T(8,128)(2,1)}, bf16[128,1024]{1,0:T(8,128)(2,1)S(1)}, u32[]{:S(2)}, u32[]{:S(2)}) collective-permute-start(bf16[128,1024]{1,0:T(8,128)(2,1)} %fusion.62), channel_id=1, source_target_pairs={{0,8},{8,0},{32,40},{40,32},{1,9},{9,1},{33,41},{41,33},{2,10},{10... | collective-permute-start | bytes 786440 | tf_op jit(solution)/shard_map/ppermute | solution.py:109
  113.4 4.0 %collective-permute-start.4 = (bf16[128,1024]{1,0:T(8,128)(2,1)}, bf16[128,1024]{1,0:T(8,128)(2,1)S(1)}, u32[]{:S(2)}, u32[]{:S(2)}) collective-permute-start(bf16[128,1024]{1,0:T(8,128)(2,1)} %fusion.64), channel_id=1, source_target_pairs={{0,32},{8,40},{32,0},{40,8},{1,33},{9,41},{33,1},{41,9},{2,34},{10... | collective-permute-start | bytes 786440 | tf_op jit(solution)/shard_map/ppermute | solution.py:109
  117.4 5.5 %collective-permute-done.6 = bf16[128,1024]{1,0:T(8,128)(2,1)S(1)} collective-permute-done((bf16[128,1024]{1,0:T(8,128)(2,1)}, bf16[128,1024]{1,0:T(8,128)(2,1)S(1)}, u32[]{:S(2)}, u32[]{:S(2)}) %collective-permute-start.6) | collective-permute-done | bytes 262176 | tf_op jit(solution)/shard_map/ppermute | solution.py:109
  122.9 1.6 collective-permute-done.5
  124.5 5.6 %collective-permute-done.4 = bf16[128,1024]{1,0:T(8,128)(2,1)S(1)} collective-permute-done((bf16[128,1024]{1,0:T(8,128)(2,1)}, bf16[128,1024]{1,0:T(8,128)(2,1)S(1)}, u32[]{:S(2)}, u32[]{:S(2)}) %collective-permute-start.4) | collective-permute-done | bytes 262176 | tf_op jit(solution)/shard_map/ppermute | solution.py:109
  130.1 1.2 add_convert_fusion.2
  131.4 0.8 copy.12
  132.1 9.2 %all-to-all-start.2 = ((bf16[64,16,128]{2,1,0:T(8,128)(2,1)}), bf16[64,16,128]{2,1,0:T(8,128)(2,1)S(1)}, u32[]{:S(2)}, u32[]{:S(2)}) async-start(bf16[64,16,128]{2,1,0:T(8,128)(2,1)} %bitcast.6), calls=%async_computation.2 | async-start | bytes 524288 | tf_op jit(solution)/shard_map/all_to_all | solution.py:125
  141.4 4.6 %fusion.35 = f32[256,1024]{1,0:T(8,128)} fusion(bf16[1024,1024]{1,0:T(8,128)(2,1)} %get-tuple-element.26, bf16[128,1024]{1,0:T(8,128)(2,1)S(1)} %copy-done.5, bf16[128,1024]{1,0:T(8,128)(2,1)S(1)} %copy-done.4, s32[256]{0:T(256)S(1)} %iota_add_fusion, pred[256]{0:T(512)(128)(4,1)S(1)} %iota_compare_fusion.13), kind=kOutput, calls=%fused_computation.49 | convolution fusion | flops 1077673984 | bytes 3671296 | tf_op jit(solution)/shard_map/dot_general | solution.py:27
  146.0 10.2 %all-to-all-done.2 = bf16[64,16,128]{2,1,0:T(8,128)(2,1)S(1)} async-done(((bf16[64,16,128]{2,1,0:T(8,128)(2,1)}), bf16[64,16,128]{2,1,0:T(8,128)(2,1)S(1)}, u32[]{:S(2)}, u32[]{:S(2)}) %all-to-all-start.2) | async-done | bytes 262176 | tf_op jit(solution)/shard_map/all_to_all | solution.py:125
  156.2 1.1 slice.59
  157.3 3.4 %collective-permute-start.8 = (bf16[128,1024]{1,0:T(8,128)(2,1)S(1)}, bf16[128,1024]{1,0:T(8,128)(2,1)S(1)}, u32[]{:S(2)}, u32[]{:S(2)}) collective-permute-start(bf16[128,1024]{1,0:T(8,128)(2,1)S(1)} %slice.59), channel_id=1, source_target_pairs={{0,8},{8,0},{1,9},{9,1},{2,10},{10,2},{3,11},{11,3},{4,12},{12,4},... | collective-permute-start | bytes 786440 | tf_op jit(solution)/shard_map/ppermute | solution.py:15
  160.8 0.6 broadcast_in_dim.2
  161.4 3.5 %all-to-all-start.3 = ((bf16[16,16,128]{2,1,0:T(8,128)(2,1)}), bf16[16,16,128]{2,1,0:T(8,128)(2,1)S(1)}, u32[]{:S(2)}, u32[]{:S(2)}) async-start(bf16[16,16,128]{2,1,0:T(8,128)(2,1)} %broadcast_in_dim.2), calls=%async_computation.3 | async-start | bytes 131072 | tf_op jit(solution)/shard_map/all_to_all | solution.py:132
  164.9 2.8 %fusion.18 = bf16[256,1024]{1,0:T(8,128)(2,1)} fusion(bf16[1024,1024]{1,0:T(8,128)(2,1)S(1)} %copy-done, f32[256,1024]{1,0:T(8,128)} %fusion.29, bf16[256,1024]{1,0:T(8,128)(2,1)S(1)} %bitcast.37, f32[256]{0:T(256)S(1)} %convert_rsqrt_fusion), kind=kOutput, calls=%fused_computation.25 | convolution fusion | flops 538181632 | bytes 4195328 | tf_op jit(solution)/shard_map/dot_general | solution.py:19
  167.7 5.7 %all-to-all-done.3 = bf16[16,16,128]{2,1,0:T(8,128)(2,1)S(1)} async-done(((bf16[16,16,128]{2,1,0:T(8,128)(2,1)}), bf16[16,16,128]{2,1,0:T(8,128)(2,1)S(1)}, u32[]{:S(2)}, u32[]{:S(2)}) %all-to-all-start.3) | async-done | bytes 65568 | tf_op jit(solution)/shard_map/all_to_all | solution.py:132
  173.4 1.8 add_convert_fusion
  175.3 0.7 copy.17
  (36 shorter events, 1.2 us)
Async XLA Ops:
  7.2 19.2 %copy-start = (bf16[1024,1024]{1,0:T(8,128)(2,1)S(1)}, bf16[1024,1024]{1,0:T(8,128)(2,1)}, u32[]{:S(2)}) copy-start(bf16[1024,1024]{1,0:T(8,128)(2,1)} %param.11) | copy-start | bytes 6291460
  7.2 15.0 %copy-start.2 = (bf16[128,1024]{1,0:T(8,128)(2,1)S(1)}, bf16[128,1024]{1,0:T(8,128)(2,1)}, u32[]{:S(2)}) copy-start(bf16[128,1024]{1,0:T(8,128)(2,1)} %param.7) | copy-start | bytes 786436
  7.2 15.0 %copy-start.3 = (bf16[128,1024]{1,0:T(8,128)(2,1)S(1)}, bf16[128,1024]{1,0:T(8,128)(2,1)}, u32[]{:S(2)}) copy-start(bf16[128,1024]{1,0:T(8,128)(2,1)} %param.6) | copy-start | bytes 786436
  7.2 66.4 %all-gather.2.cloned.1.call-start = ((), (), s32[]{:S(2)}) async-start(), calls=%async_computation.4 | async-start | bytes 4718592 | tf_op jit(solution)/shard_map/all_gather | solution.py:69
  9.3 16.9 %copy-start.6 = (s32[128,1]{0,1:T(1,128)S(1)}, s32[128,1]{0,1:T(1,128)}, u32[]{:S(2)}) copy-start(s32[128,1]{0,1:T(1,128)} %param.8) | copy-start | bytes 1540
  12.0 27.9 %all-to-all-start = ((bf16[32,8,1024]{2,1,0:T(8,128)(2,1)}), bf16[32,8,1024]{2,1,0:T(8,128)(2,1)S(1)}, u32[]{:S(2)}, u32[]{:S(2)}) async-start(bf16[32,8,1024]{2,1,0:T(8,128)(2,1)} %fusion.58), calls=%async_computation | async-start | bytes 1048576 | tf_op jit(solution)/shard_map/all_to_all | solution.py:78
  23.0 20.6 %collective-permute-start = (bf16[256,1024]{1,0:T(8,128)(2,1)}, bf16[256,1024]{1,0:T(8,128)(2,1)S(1)}, u32[]{:S(2)}, u32[]{:S(2)}) collective-permute-start(bf16[256,1024]{1,0:T(8,128)(2,1)} %pad_maximum_fusion.1), channel_id=1, source_target_pairs={{0,8},{8,0},{1,9},{9,1},{2,10},{10,2},{3,11},{11,3},{4,12},{12,4},... | collective-permute-start | bytes 1572872 | tf_op jit(solution)/shard_map/ppermute | solution.py:15
  40.2 9.4 %collective-permute-start.1 = (bf16[128,1024]{1,0:T(8,128)(2,1)S(1)}, bf16[128,1024]{1,0:T(8,128)(2,1)S(1)}, u32[]{:S(2)}, u32[]{:S(2)}) collective-permute-start(bf16[128,1024]{1,0:T(8,128)(2,1)S(1)} %convolution_convert_fusion.1), channel_id=1, source_target_pairs={{0,8},{8,0},{1,9},{9,1},{2,10},{10,2},{3,11},{11,3},{4,12},{12,4},... | collective-permute-start | bytes 786440 | tf_op jit(solution)/shard_map/ppermute | solution.py:15
  50.1 4.5 %collective-permute-start.2 = (bf16[256,512]{1,0:T(8,128)(2,1)S(1)}, bf16[256,512]{1,0:T(8,128)(2,1)S(1)}, u32[]{:S(2)}, u32[]{:S(2)}) collective-permute-start(bf16[256,512]{1,0:T(8,128)(2,1)S(1)} %fusion.20), channel_id=1, source_target_pairs={{0,16},{16,0},{1,17},{17,1},{2,18},{18,2},{3,19},{19,3},{4,20},{20... | collective-permute-start | bytes 786440 | tf_op jit(solution)/shard_map/ppermute | solution.py:15
  83.0 6.6 %copy-start.1 = (bf16[512,512]{1,0:T(8,128)(2,1)S(1)}, bf16[512,512]{1,0:T(8,128)(2,1)}, u32[]{:S(2)}) copy-start(bf16[512,512]{1,0:T(8,128)(2,1)} %pad_maximum_fusion.6) | copy-start | bytes 1572868
  84.5 5.1 %collective-permute-start.3 = (bf16[256,1024]{1,0:T(8,128)(2,1)S(1)}, bf16[256,1024]{1,0:T(8,128)(2,1)S(1)}, u32[]{:S(2)}, u32[]{:S(2)}) collective-permute-start(bf16[256,1024]{1,0:T(8,128)(2,1)S(1)} %multiply_convert_fusion.1), channel_id=1, source_target_pairs={{0,16},{16,0},{1,17},{17,1},{2,18},{18,2},{3,19},{19,3},{4,20},{20... | collective-permute-start | bytes 1572872 | tf_op jit(solution)/shard_map/ppermute | solution.py:15
  86.4 10.6 %collective-permute-start.7 = (bf16[128,1024]{1,0:T(8,128)(2,1)S(1)}, bf16[128,1024]{1,0:T(8,128)(2,1)S(1)}, u32[]{:S(2)}, u32[]{:S(2)}) collective-permute-start(bf16[128,1024]{1,0:T(8,128)(2,1)S(1)} %slice.60), channel_id=1, source_target_pairs={{0,8},{8,0},{1,9},{9,1},{2,10},{10,2},{3,11},{11,3},{4,12},{12,4},... | collective-permute-start | bytes 786440 | tf_op jit(solution)/shard_map/ppermute | solution.py:15
  98.1 43.2 %copy-start.4 = (bf16[128,1024]{1,0:T(8,128)(2,1)S(1)}, bf16[128,1024]{1,0:T(8,128)(2,1)}, u32[]{:S(2)}) copy-start(bf16[128,1024]{1,0:T(8,128)(2,1)} %param.6) | copy-start | bytes 786436
  98.1 43.2 %copy-start.5 = (bf16[128,1024]{1,0:T(8,128)(2,1)S(1)}, bf16[128,1024]{1,0:T(8,128)(2,1)}, u32[]{:S(2)}) copy-start(bf16[128,1024]{1,0:T(8,128)(2,1)} %get-tuple-element.35) | copy-start | bytes 786436
  98.1 33.2 %all-to-all-start.1 = ((bf16[32,8,1024]{2,1,0:T(8,128)(2,1)}), bf16[32,8,1024]{2,1,0:T(8,128)(2,1)S(1)}, u32[]{:S(2)}, u32[]{:S(2)}) async-start(bf16[32,8,1024]{2,1,0:T(8,128)(2,1)} %fusion.19), calls=%async_computation.1 | async-start | bytes 1048576 | tf_op jit(solution)/shard_map/all_to_all | solution.py:117
  108.1 14.8 %collective-permute-start.6 = (bf16[128,1024]{1,0:T(8,128)(2,1)}, bf16[128,1024]{1,0:T(8,128)(2,1)S(1)}, u32[]{:S(2)}, u32[]{:S(2)}) collective-permute-start(bf16[128,1024]{1,0:T(8,128)(2,1)} %fusion.60), channel_id=1, source_target_pairs={{0,40},{8,32},{32,8},{40,0},{1,41},{9,33},{33,9},{41,1},{2,42},{10... | collective-permute-start | bytes 786440 | tf_op jit(solution)/shard_map/ppermute | solution.py:109
  110.1 14.5 %collective-permute-start.5 = (bf16[128,1024]{1,0:T(8,128)(2,1)}, bf16[128,1024]{1,0:T(8,128)(2,1)S(1)}, u32[]{:S(2)}, u32[]{:S(2)}) collective-permute-start(bf16[128,1024]{1,0:T(8,128)(2,1)} %fusion.62), channel_id=1, source_target_pairs={{0,8},{8,0},{32,40},{40,32},{1,9},{9,1},{33,41},{41,33},{2,10},{10... | collective-permute-start | bytes 786440 | tf_op jit(solution)/shard_map/ppermute | solution.py:109
  113.4 16.7 %collective-permute-start.4 = (bf16[128,1024]{1,0:T(8,128)(2,1)}, bf16[128,1024]{1,0:T(8,128)(2,1)S(1)}, u32[]{:S(2)}, u32[]{:S(2)}) collective-permute-start(bf16[128,1024]{1,0:T(8,128)(2,1)} %fusion.64), channel_id=1, source_target_pairs={{0,32},{8,40},{32,0},{40,8},{1,33},{9,41},{33,1},{41,9},{2,34},{10... | collective-permute-start | bytes 786440 | tf_op jit(solution)/shard_map/ppermute | solution.py:109
  132.1 24.1 %all-to-all-start.2 = ((bf16[64,16,128]{2,1,0:T(8,128)(2,1)}), bf16[64,16,128]{2,1,0:T(8,128)(2,1)S(1)}, u32[]{:S(2)}, u32[]{:S(2)}) async-start(bf16[64,16,128]{2,1,0:T(8,128)(2,1)} %bitcast.6), calls=%async_computation.2 | async-start | bytes 524288 | tf_op jit(solution)/shard_map/all_to_all | solution.py:125
  157.3 16.1 %collective-permute-start.8 = (bf16[128,1024]{1,0:T(8,128)(2,1)S(1)}, bf16[128,1024]{1,0:T(8,128)(2,1)S(1)}, u32[]{:S(2)}, u32[]{:S(2)}) collective-permute-start(bf16[128,1024]{1,0:T(8,128)(2,1)S(1)} %slice.59), channel_id=1, source_target_pairs={{0,8},{8,0},{1,9},{9,1},{2,10},{10,2},{3,11},{11,3},{4,12},{12,4},... | collective-permute-start | bytes 786440 | tf_op jit(solution)/shard_map/ppermute | solution.py:15
  161.4 12.0 %all-to-all-start.3 = ((bf16[16,16,128]{2,1,0:T(8,128)(2,1)}), bf16[16,16,128]{2,1,0:T(8,128)(2,1)S(1)}, u32[]{:S(2)}, u32[]{:S(2)}) async-start(bf16[16,16,128]{2,1,0:T(8,128)(2,1)} %broadcast_in_dim.2), calls=%async_computation.3 | async-start | bytes 131072 | tf_op jit(solution)/shard_map/all_to_all | solution.py:132
Sparse Core Ops, SparseCore 0:
  10.7 62.8 all-gather.1
